TPU v7x, 32 devices: a whole 2x2x4 slice. The times are simulated.
32 devices in a mesh: seq: 4 (over z), shard: 8 (over y, x, core).
Axes of the slice: x: 2, y: 2, z: 4, core: 2. Of those that a mesh axis runs over, the one named last changes fastest.
Arguments:
- tokens_in: bfloat16 [8, 512, 1024], P('shard', 'seq'), may hold values from -6 to 6
- out_grad: bfloat16 [8, 512, 1024], P('shard', 'seq'), may hold values from -6 to 6
- segments: int32 [8, 512], P('shard'), may hold values from 0 to 3, never falling along the last dimension, each value on 1 to 256 neighbouring positions
- w_qkv: float32 [1024, 3072], P(('seq', 'shard'))
- w_out: float32 [1024, 1024], P(('seq', 'shard')), may hold values from -0.375 to 0.375
- w_up: float32 [1024, 4096], P(('seq', 'shard')), may hold values from -0.1875 to 0.1875
- w_down: float32 [1024, 4096], P(('seq', 'shard')), may hold values from -0.09375 to 0.09375
- vectors: float32 [12288], P(('seq', 'shard'))
- mom_qkv: float32 [1024, 3072], P(('seq', 'shard')), may hold values from -56 to 56
- mom_out: float32 [1024, 1024], P(('seq', 'shard')), may hold values from -56 to 56
- mom_up: float32 [1024, 4096], P(('seq', 'shard')), may hold values from -40 to 40
- mom_down: float32 [1024, 4096], P(('seq', 'shard')), may hold values from -56 to 56
- mom_vectors: float32 [12288], P(('seq', 'shard')), may hold values from -80 to 80
Outputs:
- block_out: bfloat16 [8, 512, 1024], P('shard', 'seq')
- grad_inputs: float32 [8, 512, 1024], P('shard', 'seq')
- grad_qkv: float32 [1024, 3072], P(('seq', 'shard'))
- grad_out: float32 [1024, 1024], P(('seq', 'shard'))
- grad_up: float32 [1024, 4096], P(('seq', 'shard'))
- grad_down: float32 [1024, 4096], P(('seq', 'shard'))
- grad_vectors: float32 [12288], P(('seq', 'shard'))
- new_qkv: float32 [1024, 3072], P(('seq', 'shard'))
- new_out: float32 [1024, 1024], P(('seq', 'shard'))
- new_up: float32 [1024, 4096], P(('seq', 'shard'))
- new_down: float32 [1024, 4096], P(('seq', 'shard'))
- new_vectors: float32 [12288], P(('seq', 'shard'))
- next_mom_qkv: float32 [1024, 3072], P(('seq', 'shard'))
- next_mom_out: float32 [1024, 1024], P(('seq', 'shard'))
- next_mom_up: float32 [1024, 4096], P(('seq', 'shard'))
- next_mom_down: float32 [1024, 4096], P(('seq', 'shard'))
- next_mom_vectors: float32 [12288], P(('seq', 'shard'))
Inputs may be any that keep to these rules, and one draw needn't show every extreme that they name: `segments`: each row's document ids never fall; a document holds at most 256 positions.
All inputs are finite; a program needn't handle non-finite values.
Results may differ from a plain program's by a relative error of at most 0.012.
Values may be sent and summed in bfloat16 or wider, within the bound.
No kernel may reach another device: no remote copies, remote signals or barrier semaphores. Data moves between devices by JAX's collectives and lax.ppermute only.
A program may use at most 192 MiB of HBM per device.

v0:
```python
import math

import jax
import jax.numpy as jnp
from jax import lax
from jax.sharding import PartitionSpec as P

D = 1024
H = 16
HD = 64
FF = 4096
NS_ITERS = 3


newton_coefs = (3.4445, -4.775, 2.0315)
momentum_decay = 0.9
matrix_rate = 0.1
vector_rate = 0.2
highest = lax.Precision.HIGHEST


def for_sending(array):

    def short(part):
        return part.astype(jnp.bfloat16) if part.dtype == jnp.float32 else part

    return jax.tree.map(short, array)


def layer_norm(values, gain_vec, shift_vec):
    center = values - jnp.mean(values, axis=-1, keepdims=True)
    spread = jnp.mean(center * center, axis=-1, keepdims=True)
    return center * lax.rsqrt(spread + 1e-05) * gain_vec + shift_vec


def gelu_tanh(values):
    return jax.nn.gelu(values, approximate=True)


def unpack(flat_vec):
    rows = flat_vec.reshape(12, D)
    return (
        rows[0],
        rows[1],
        rows[2],
        rows[3],
        rows[4],
        rows[5],
        rows[6],
        rows[7:11].reshape(FF),
        rows[11],
    )


def head_slopes(first_head, head_count):
    heads = (first_head + jnp.arange(head_count)).astype(jnp.float32)
    return jnp.exp2(-8.0 * (heads + 1.0) / H)


def block_scores(query, key_rows, query_seg, key_seg, slopes, begin_row):
    scores = jnp.einsum(
        "qhd,khd->hqk", query, key_rows, preferred_element_type=jnp.float32
    ) * HD ** (-0.5)
    query_pos = begin_row + jnp.arange(query.shape[0])
    key_pos = jnp.arange(key_rows.shape[0])
    distance = (query_pos[:, None] - key_pos[None, :]).astype(jnp.float32)
    scores = scores - slopes[:, None, None] * distance[None]
    allowed = (distance >= 0) & (query_seg[:, None] == key_seg[None, :])
    return jnp.where(allowed[None], scores, -1e30)


def pad_columns(matrix):
    return jnp.pad(matrix, ((0, 0), (0, FF - matrix.shape[1])))


def orthogonalize(column_block):
    current = column_block
    for sweep_index in range(NS_ITERS):
        gram_matrix = lax.psum(
            jnp.dot(current, current.T, precision=highest).astype(jnp.bfloat16), "seq"
        ).astype(jnp.float32)
        if sweep_index == 0:
            factor = 1.0 / (jnp.sqrt(jnp.trace(gram_matrix)) + 1e-07)
            current = current * factor
            gram_matrix = gram_matrix * (factor * factor)
        one_product = jnp.dot(gram_matrix, current, precision=highest)
        two_product = jnp.dot(gram_matrix, one_product, precision=highest)
        current = (
            newton_coefs[0] * current
            + newton_coefs[1] * one_product
            + newton_coefs[2] * two_product
        )
    return current


def per_device(
    tokens_in,
    out_grad,
    segments,
    w_qkv,
    w_out,
    w_up,
    w_down,
    vectors,
    mom_qkv,
    mom_out,
    mom_up,
    mom_down,
    mom_vectors,
):
    full_qkv, full_out, full_up, full_down, full_vec = (
        lax.all_gather(w_qkv.astype(jnp.bfloat16), ("seq", "shard"), axis=0, tiled=True),
        lax.all_gather(w_out.astype(jnp.bfloat16), ("seq", "shard"), axis=0, tiled=True),
        lax.all_gather(w_up.astype(jnp.bfloat16), ("seq", "shard"), axis=0, tiled=True),
        lax.all_gather(w_down.astype(jnp.bfloat16), ("seq", "shard"), axis=0, tiled=True),
        lax.all_gather(vectors.astype(jnp.bfloat16), ("seq", "shard"), axis=0, tiled=True),
    )
    (
        gain_one,
        shift_one,
        bias_query,
        bias_value,
        bias_out,
        gain_two,
        shift_two,
        bias_up,
        bias_down,
    ) = unpack(full_vec.astype(jnp.float32))
    groups = lax.axis_size("seq")
    shards = lax.axis_size("shard")
    length = tokens_in.shape[1]
    seq_span = length * groups
    local_heads = H // groups
    half_rows = seq_span // 2
    pair_shape = (length, H // 2, 2 * HD)
    head_shape = (seq_span, local_heads, HD)
    local_pairs = (seq_span, local_heads // 2, 2 * HD)
    residual = tokens_in[0].astype(jnp.float32)
    hidden_one = layer_norm(residual, gain_one, shift_one).astype(jnp.bfloat16)
    qkv_bias = jnp.concatenate([bias_query, jnp.zeros((D,), jnp.float32), bias_value])
    qkv_mixed = jnp.dot(hidden_one, full_qkv, preferred_element_type=jnp.float32) + qkv_bias
    query_rows = qkv_mixed[:, :D].astype(jnp.bfloat16).reshape(pair_shape)
    key_rows = qkv_mixed[:, D : 2 * D].astype(jnp.bfloat16).reshape(pair_shape)
    value_rows = qkv_mixed[:, 2 * D :].astype(jnp.bfloat16).reshape(pair_shape)
    head_query, head_keys, head_values = (
        lax.all_to_all(query_rows, "seq", split_axis=1, concat_axis=0, tiled=True),
        lax.all_to_all(key_rows, "seq", split_axis=1, concat_axis=0, tiled=True),
        lax.all_to_all(value_rows, "seq", split_axis=1, concat_axis=0, tiled=True),
    )
    head_query = head_query.reshape(head_shape)
    head_keys = head_keys.reshape(head_shape)
    head_values = head_values.reshape(head_shape)
    seg_row = segments[0]
    slopes = head_slopes(lax.axis_index("seq") * local_heads, local_heads)
    attended_parts = []
    logsum_parts = []
    for part_index in range(2):
        begin_row = part_index * half_rows
        end_row = begin_row + half_rows
        scores = block_scores(
            head_query[begin_row:end_row],
            head_keys[:end_row],
            seg_row[begin_row:end_row],
            seg_row[:end_row],
            slopes,
            begin_row,
        )
        row_max = jnp.max(scores, axis=-1, keepdims=True)
        exp_terms = jnp.exp(scores - row_max)
        row_total = jnp.sum(exp_terms, axis=-1, keepdims=True)
        logsum_parts.append(row_max + jnp.log(row_total))
        prob_rows = (exp_terms / row_total).astype(jnp.bfloat16)
        attended_parts.append(
            jnp.einsum(
                "hqk,khd->qhd", prob_rows, head_values[:end_row], preferred_element_type=jnp.float32
            ).astype(jnp.bfloat16)
        )
    attended_heads = jnp.concatenate(attended_parts, axis=0).reshape(local_pairs)
    attended = lax.all_to_all(
        attended_heads, "seq", split_axis=0, concat_axis=1, tiled=True
    ).reshape(length, D)
    middle = residual + jnp.dot(attended, full_out, preferred_element_type=jnp.float32) + bias_out
    hidden_two = layer_norm(middle, gain_two, shift_two).astype(jnp.bfloat16)
    before = jnp.dot(hidden_two, full_up, preferred_element_type=jnp.float32) + bias_up
    active = gelu_tanh(before).astype(jnp.bfloat16)
    block_rows = (
        middle + jnp.dot(active, full_down.T, preferred_element_type=jnp.float32) + bias_down
    ).astype(jnp.bfloat16)
    cotangent = out_grad[0]
    upstream = cotangent.astype(jnp.float32)
    grad_down = jnp.dot(cotangent.T, active, preferred_element_type=jnp.float32)
    grad_active = jnp.dot(cotangent, full_down, preferred_element_type=jnp.float32)
    grad_before = jax.vjp(gelu_tanh, before)[1](grad_active)[0]
    grad_before_b = grad_before.astype(jnp.bfloat16)
    grad_up = jnp.dot(hidden_two.T, grad_before_b, preferred_element_type=jnp.float32)
    grad_hidden_two = jnp.dot(grad_before_b, full_up.T, preferred_element_type=jnp.float32)
    middle_part, grad_gain_two, grad_shift_two = jax.vjp(layer_norm, middle, gain_two, shift_two)[
        1
    ](grad_hidden_two)
    grad_middle = upstream + middle_part
    grad_middle_b = grad_middle.astype(jnp.bfloat16)
    grad_out = jnp.dot(attended.T, grad_middle_b, preferred_element_type=jnp.float32)
    grad_attended = (
        jnp.dot(grad_middle_b, full_out.T, preferred_element_type=jnp.float32)
        .astype(jnp.bfloat16)
        .reshape(pair_shape)
    )
    head_grad = lax.all_to_all(
        grad_attended, "seq", split_axis=1, concat_axis=0, tiled=True
    ).reshape(head_shape)
    grad_key_acc = jnp.zeros(head_shape, jnp.float32)
    grad_value_acc = jnp.zeros(head_shape, jnp.float32)
    grad_query_parts = []
    for part_index in range(2):
        begin_row = part_index * half_rows
        end_row = begin_row + half_rows
        scores = block_scores(
            head_query[begin_row:end_row],
            head_keys[:end_row],
            seg_row[begin_row:end_row],
            seg_row[:end_row],
            slopes,
            begin_row,
        )
        prob_again = jnp.exp(scores - logsum_parts[part_index])
        prob_again_b = prob_again.astype(jnp.bfloat16)
        grad_rows_block = head_grad[begin_row:end_row]
        grad_value_acc = grad_value_acc.at[:end_row].add(
            jnp.einsum(
                "hqk,qhd->khd", prob_again_b, grad_rows_block, preferred_element_type=jnp.float32
            )
        )
        grad_probs = jnp.einsum(
            "qhd,khd->hqk",
            grad_rows_block,
            head_values[:end_row],
            preferred_element_type=jnp.float32,
        )
        row_inner = jnp.sum(prob_again * grad_probs, axis=-1, keepdims=True)
        grad_scores = (prob_again * (grad_probs - row_inner) * HD ** (-0.5)).astype(jnp.bfloat16)
        grad_query_parts.append(
            jnp.einsum(
                "hqk,khd->qhd", grad_scores, head_keys[:end_row], preferred_element_type=jnp.float32
            ).astype(jnp.bfloat16)
        )
        grad_key_acc = grad_key_acc.at[:end_row].add(
            jnp.einsum(
                "hqk,qhd->khd",
                grad_scores,
                head_query[begin_row:end_row],
                preferred_element_type=jnp.float32,
            )
        )
    grad_query_heads = jnp.concatenate(grad_query_parts, axis=0).reshape(local_pairs)
    back_query, back_keys, back_values = (
        lax.all_to_all(grad_query_heads, "seq", split_axis=0, concat_axis=1, tiled=True),
        lax.all_to_all(
            grad_key_acc.astype(jnp.bfloat16).reshape(local_pairs),
            "seq",
            split_axis=0,
            concat_axis=1,
            tiled=True,
        ),
        lax.all_to_all(
            grad_value_acc.astype(jnp.bfloat16).reshape(local_pairs),
            "seq",
            split_axis=0,
            concat_axis=1,
            tiled=True,
        ),
    )
    back_query = back_query.reshape(length, D)
    back_values = back_values.reshape(length, D)
    grad_mixed = jnp.concatenate([back_query, back_keys.reshape(length, D), back_values], axis=1)
    grad_qkv = jnp.dot(hidden_one.T, grad_mixed, preferred_element_type=jnp.float32)
    grad_hidden_one = jnp.dot(grad_mixed, full_qkv.T, preferred_element_type=jnp.float32)
    input_part, grad_gain_one, grad_shift_one = jax.vjp(layer_norm, residual, gain_one, shift_one)[
        1
    ](grad_hidden_one)
    grad_rows = grad_middle + input_part
    grad_vec = jnp.concatenate(
        [
            grad_gain_one,
            grad_shift_one,
            jnp.sum(back_query.astype(jnp.float32), axis=0),
            jnp.sum(back_values.astype(jnp.float32), axis=0),
            jnp.sum(grad_middle, axis=0),
            grad_gain_two,
            grad_shift_two,
            jnp.sum(grad_before, axis=0),
            jnp.sum(upstream, axis=0),
        ]
    )
    shard_qkv, shard_out, shard_up, shard_down, shard_vec = (
        lax.psum_scatter(grad_qkv, ("seq", "shard"), scatter_dimension=0, tiled=True),
        lax.psum_scatter(grad_out, ("seq", "shard"), scatter_dimension=0, tiled=True),
        lax.psum_scatter(grad_up, ("seq", "shard"), scatter_dimension=0, tiled=True),
        lax.psum_scatter(grad_down, ("seq", "shard"), scatter_dimension=0, tiled=True),
        lax.psum_scatter(grad_vec, ("seq", "shard"), scatter_dimension=0, tiled=True),
    )
    next_qkv = momentum_decay * mom_qkv + shard_qkv
    next_out = momentum_decay * mom_out + shard_out
    next_up = momentum_decay * mom_up + shard_up
    next_down = momentum_decay * mom_down + shard_down
    next_vec = momentum_decay * mom_vectors + shard_vec
    moments = (next_qkv, next_out, next_up, next_down)
    owner_table = jnp.arange(4) * shards // 4
    owned_flags = (owner_table == lax.axis_index("shard")).astype(jnp.float32)
    gathered = (
        lax.all_gather(moments[0].astype(jnp.bfloat16), "shard", axis=0, tiled=True).astype(
            jnp.float32
        ),
        lax.all_gather(moments[1].astype(jnp.bfloat16), "shard", axis=0, tiled=True).astype(
            jnp.float32
        ),
        lax.all_gather(moments[2].astype(jnp.bfloat16), "shard", axis=0, tiled=True).astype(
            jnp.float32
        ),
        lax.all_gather(moments[3].astype(jnp.bfloat16), "shard", axis=0, tiled=True).astype(
            jnp.float32
        ),
    )
    stacked_rows = jnp.stack([pad_columns(moment) for moment in gathered])
    chosen = jnp.einsum("m,mrc->rc", owned_flags, stacked_rows, precision=highest)
    column_block = lax.all_to_all(
        for_sending(chosen), "seq", split_axis=1, concat_axis=0, tiled=True
    ).astype(chosen.dtype)
    result = orthogonalize(column_block)
    back_rows = lax.all_to_all(
        for_sending(result), "seq", split_axis=0, concat_axis=1, tiled=True
    ).astype(result.dtype)
    stacked = owned_flags[:, None, None] * back_rows[None]
    pieces = lax.psum_scatter(
        stacked.astype(jnp.bfloat16), "shard", scatter_dimension=1, tiled=True
    ).astype(jnp.float32)
    new_qkv = w_qkv - matrix_rate * 0.2 * math.sqrt(3 * D) * pieces[0][:, : 3 * D]
    new_out = w_out - matrix_rate * 0.2 * math.sqrt(D) * pieces[1][:, :D]
    new_up = w_up - matrix_rate * 0.2 * math.sqrt(FF) * pieces[2]
    new_down = w_down - matrix_rate * 0.2 * math.sqrt(FF) * pieces[3]
    total_tokens = length * groups * shards
    new_vec = vectors - vector_rate / math.sqrt(total_tokens) * next_vec
    return (
        block_rows[None],
        grad_rows[None],
        shard_qkv,
        shard_out,
        shard_up,
        shard_down,
        shard_vec,
        new_qkv,
        new_out,
        new_up,
        new_down,
        new_vec,
        next_qkv,
        next_out,
        next_up,
        next_down,
        next_vec,
    )


def solution(mesh):
    return jax.shard_map(
        per_device,
        mesh=mesh,
        in_specs=(
            P("shard", "seq", None),
            P("shard", "seq", None),
            P("shard", None),
            P(("seq", "shard"), None),
            P(("seq", "shard"), None),
            P(("seq", "shard"), None),
            P(("seq", "shard"), None),
            P(("seq", "shard")),
            P(("seq", "shard"), None),
            P(("seq", "shard"), None),
            P(("seq", "shard"), None),
            P(("seq", "shard"), None),
            P(("seq", "shard")),
        ),
        out_specs=(
            P("shard", "seq", None),
            P("shard", "seq", None),
            P(("seq", "shard"), None),
            P(("seq", "shard"), None),
            P(("seq", "shard"), None),
            P(("seq", "shard"), None),
            P(("seq", "shard")),
            P(("seq", "shard"), None),
            P(("seq", "shard"), None),
            P(("seq", "shard"), None),
            P(("seq", "shard"), None),
            P(("seq", "shard")),
            P(("seq", "shard"), None),
            P(("seq", "shard"), None),
            P(("seq", "shard"), None),
            P(("seq", "shard"), None),
            P(("seq", "shard")),
        ),
        check_vma=False,
    )
```

profile of v0, /device:TPU:0, one launch (start us, length us, event | category | flops | bytes accessed | tf_op | source)
XLA Modules:
  0.0 1761.2 jit_solution(6395018226679227869)
XLA Ops:
  13.4 43.5 %all-gather = bf16[32,1,384]{2,1,0:T(2,128)(2,1)S(1)} all-gather(bf16[1,1,384]{2,1,0:T(2,128)(2,1)S(1)} %reshape.515), channel_id=1, replica_groups=mesh['seq'=4,'shard'=8] {'seq','shard'}, dimensions={0}, use_global_device_ids=true | all-gather | bytes 25344 | tf_op jit(solution)/shard_map/all_gather | solution.py:116
  57.9 25.9 %all-gather.9.cloned.1.call-done = bf16[1024,3072]{1,0:T(8,128)(2,1)} async-done(((bf16[32,3072]{1,0:T(8,128)(2,1)}), bf16[1024,3072]{1,0:T(8,128)(2,1)}) %all-gather.9.cloned.1.call-update) | async-done | bytes 6291472 | tf_op jit(solution)/shard_map/all_gather | solution.py:112
  146.8 78.4 %all-gather.13.cloned.1.call-done = bf16[1024,4096]{1,0:T(8,128)(2,1)} async-done(((bf16[32,4096]{1,0:T(8,128)(2,1)}), bf16[1024,4096]{1,0:T(8,128)(2,1)}) %all-gather.13.cloned.1.call-update) | async-done | bytes 8388624 | tf_op jit(solution)/shard_map/all_gather | solution.py:114
  230.0 74.6 %all-gather.15.cloned.1.call-done = bf16[1024,4096]{1,0:T(8,128)(2,1)} async-done(((bf16[32,4096]{1,0:T(8,128)(2,1)}), bf16[1024,4096]{1,0:T(8,128)(2,1)}) %all-gather.15.cloned.1.call-update) | async-done | bytes 8388624 | tf_op jit(solution)/shard_map/all_gather | solution.py:115
  435.1 131.9 %reduce-scatter.6.cloned.1.call-done = f32[32,3072]{1,0:T(8,128)} async-done(((f32[1024,3072]{1,0:T(8,128)}), f32[32,3072]{1,0:T(8,128)}) %reduce-scatter.6.cloned.1.call-update) | async-done | bytes 393232 | tf_op jit(solution)/shard_map/reduce_scatter | solution.py:295
  568.9 182.9 %reduce-scatter.12.cloned.1.call-done = f32[32,4096]{1,0:T(8,128)} async-done(((f32[1024,4096]{1,0:T(8,128)}), f32[32,4096]{1,0:T(8,128)}) %reduce-scatter.12.cloned.1.call-update) | async-done | bytes 524304 | tf_op jit(solution)/shard_map/reduce_scatter | solution.py:298
  753.8 185.3 %reduce-scatter.10.cloned.1.call-done = f32[32,4096]{1,0:T(8,128)} async-done(((f32[1024,4096]{1,0:T(8,128)}), f32[32,4096]{1,0:T(8,128)}) %reduce-scatter.10.cloned.1.call-update) | async-done | bytes 524304 | tf_op jit(solution)/shard_map/reduce_scatter | solution.py:297
  941.1 143.4 %reduce-scatter.8.cloned.1.call-done = f32[32,1024]{1,0:T(8,128)} async-done(((f32[1024,1024]{1,0:T(8,128)}), f32[32,1024]{1,0:T(8,128)}) %reduce-scatter.8.cloned.1.call-update) | async-done | bytes 131088 | tf_op jit(solution)/shard_map/reduce_scatter | solution.py:296
  1096.2 12.1 all-gather.17.cloned.1.call-done
  1111.3 27.4 %all-gather.21.cloned.1.call-done = bf16[256,4096]{1,0:T(8,128)(2,1)} async-done(((bf16[32,4096]{1,0:T(8,128)(2,1)}), bf16[256,4096]{1,0:T(8,128)(2,1)}) %all-gather.21.cloned.1.call-update) | async-done | bytes 2097168 | tf_op jit(solution)/shard_map/all_gather | solution.py:319
  1138.7 30.6 %all-gather.19.cloned.1.call-done = bf16[256,4096]{1,0:T(8,128)(2,1)} async-done(((bf16[32,4096]{1,0:T(8,128)(2,1)}), bf16[256,4096]{1,0:T(8,128)(2,1)}) %all-gather.19.cloned.1.call-update) | async-done | bytes 2097168 | tf_op jit(solution)/shard_map/all_gather | solution.py:316
  1189.3 53.1 %all_to_all.152 = bf16[256,4,1024]{0,2,1:T(8,128)(2,1)} all-to-all(bf16[256,4,1024]{0,2,1:T(8,128)(2,1)S(1)} %bitcast.236), channel_id=1, replica_groups=mesh['seq'=4,'shard'=8] {'seq'}, dimensions={1} | all-to-all | bytes 4194304 | tf_op jit(solution)/shard_map/all_to_all | solution.py:325
  1249.4 84.6 %all-reduce.9.cloned.1.call-done = bf16[1024,1024]{1,0:T(8,128)(2,1)} async-done(((bf16[1024,1024]{1,0:T(8,128)(2,1)}), bf16[1024,1024]{1,0:T(8,128)(2,1)}) %all-reduce.9.cloned.1.call-update) | async-done | bytes 2097168 | tf_op jit(solution)/shard_map/psum | solution.py:79
  1337.3 15.6 fusion.5
  1352.9 14.5 multiply_add_fusion.1
  1369.3 14.9 convolution_convert_fusion.1
  1384.3 85.6 %all-reduce.11.cloned.1.call-done = bf16[1024,1024]{1,0:T(8,128)(2,1)} async-done(((bf16[1024,1024]{1,0:T(8,128)(2,1)}), bf16[1024,1024]{1,0:T(8,128)(2,1)}) %all-reduce.11.cloned.1.call-update) | async-done | bytes 2097168 | tf_op jit(solution)/shard_map/psum | solution.py:79
  1469.9 10.5 fusion.154
  1490.1 14.7 convolution_convert_fusion
  1504.8 85.6 %all-reduce.13.cloned.1.call-done = bf16[1024,1024]{1,0:T(8,128)(2,1)} async-done(((bf16[1024,1024]{1,0:T(8,128)(2,1)}), bf16[1024,1024]{1,0:T(8,128)(2,1)}) %all-reduce.13.cloned.1.call-update) | async-done | bytes 2097168 | tf_op jit(solution)/shard_map/psum | solution.py:79
  1590.4 10.4 fusion.155
  1615.1 48.4 %all-to-all-done.9 = bf16[4,256,1024]{1,2,0:T(8,128)(2,1)S(1)} async-done(((bf16[4,256,1024]{1,2,0:T(8,128)(2,1)}), bf16[4,256,1024]{1,2,0:T(8,128)(2,1)S(1)}, u32[]{:S(2)}, u32[]{:S(2)}) %all-to-all-start.9) | async-done | bytes 2097184 | tf_op jit(solution)/shard_map/all_to_all | solution.py:329
  1694.0 38.3 %all-reduce.4 = f32[12288]{0:T(1024)S(1)} all-reduce(f32[12288]{0:T(1024)S(1)} %constant_dynamic-update-slice_fusion), channel_id=6, replica_groups=mesh['seq'=4,'shard'=8] {'seq','shard'}, use_global_device_ids=true, to_apply=%region_27.28.clone | all-reduce | flops 12288 | bytes 98304
  1733.0 17.1 reduce-scatter.14.cloned.1.call-done
  (321 shorter events, 315.8 us)
Async XLA Ops:
  7.2 76.5 %all-gather.9.cloned.1.call-start = ((), (), s32[]{:S(2)}) async-start(), calls=%async_computation.15 | async-start | bytes 6488064 | tf_op jit(solution)/shard_map/all_gather | solution.py:112
  9.0 135.4 %all-gather.11.cloned.1.call-start = ((), (), s32[]{:S(2)}) async-start(), calls=%async_computation.16 | async-start | bytes 2162688 | tf_op jit(solution)/shard_map/all_gather | solution.py:113
  10.7 214.5 %all-gather.13.cloned.1.call-start = ((), (), s32[]{:S(2)}) async-start(), calls=%async_computation.17 | async-start | bytes 8650752 | tf_op jit(solution)/shard_map/all_gather | solution.py:114
  12.5 292.1 %all-gather.15.cloned.1.call-start = ((), (), s32[]{:S(2)}) async-start(), calls=%async_computation.18 | async-start | bytes 8650752 | tf_op jit(solution)/shard_map/all_gather | solution.py:115
  88.4 13.7 all-to-all-start.2
  102.1 11.2 all-to-all-start
  113.3 10.8 all-to-all-start.1
  129.2 12.9 all-to-all-start.3
  317.0 13.7 all-to-all-start.4
  346.0 21.2 %all-to-all-start.7 = ((bf16[512,2,128]{2,1,0:T(2,128)(2,1)}), bf16[512,2,128]{2,1,0:T(2,128)(2,1)}, u32[]{:S(2)}, u32[]{:S(2)}) async-start(bf16[512,2,128]{2,1,0:T(2,128)(2,1)} %copy.120), calls=%async_computation.7 | async-start | bytes 524288 | tf_op jit(solution)/shard_map/all_to_all | solution.py:264
  367.2 20.6 %all-to-all-start.5 = ((bf16[512,2,128]{2,1,0:T(2,128)(2,1)}), bf16[512,2,128]{2,1,0:T(2,128)(2,1)}, u32[]{:S(2)}, u32[]{:S(2)}) async-start(bf16[512,2,128]{2,1,0:T(2,128)(2,1)} %copy.112), calls=%async_computation.5 | async-start | bytes 524288 | tf_op jit(solution)/shard_map/all_to_all | solution.py:256
  387.8 12.1 all-to-all-start.6
  392.9 174.1 %reduce-scatter.6.cloned.1.call-start = ((), (), s32[]{:S(2)}) async-start(), calls=%async_computation.19 | async-start | bytes 12976128 | tf_op jit(solution)/shard_map/reduce_scatter | solution.py:295
  410.9 340.9 %reduce-scatter.12.cloned.1.call-start = ((), (), s32[]{:S(2)}) async-start(), calls=%async_computation.22 | async-start | bytes 17301504 | tf_op jit(solution)/shard_map/reduce_scatter | solution.py:298
  420.7 518.4 %reduce-scatter.10.cloned.1.call-start = ((), (), s32[]{:S(2)}) async-start(), calls=%async_computation.21 | async-start | bytes 17301504 | tf_op jit(solution)/shard_map/reduce_scatter | solution.py:297
  431.1 653.5 %reduce-scatter.8.cloned.1.call-start = ((), (), s32[]{:S(2)}) async-start(), calls=%async_computation.20 | async-start | bytes 4325376 | tf_op jit(solution)/shard_map/reduce_scatter | solution.py:296
  435.0 673.3 %all-gather.17.cloned.1.call-start = ((), (), s32[]{:S(2)}) async-start(), calls=%async_computation.23 | async-start | bytes 1769472 | tf_op jit(solution)/shard_map/all_gather | solution.py:310
  568.9 569.9 %all-gather.21.cloned.1.call-start = ((), (), s32[]{:S(2)}) async-start(), calls=%async_computation.25 | async-start | bytes 2359296 | tf_op jit(solution)/shard_map/all_gather | solution.py:319
  753.8 415.5 %all-gather.19.cloned.1.call-start = ((), (), s32[]{:S(2)}) async-start(), calls=%async_computation.24 | async-start | bytes 2359296 | tf_op jit(solution)/shard_map/all_gather | solution.py:316
  941.1 392.9 %all-reduce.9.cloned.1.call-start = ((), (), s32[]{:S(2)}) async-start(), calls=%async_computation.26 | async-start | bytes 4194304 | tf_op jit(solution)/shard_map/psum | solution.py:79
  1249.2 220.6 %all-reduce.11.cloned.1.call-start = ((), (), s32[]{:S(2)}) async-start(), calls=%async_computation.27 | async-start | bytes 4194304 | tf_op jit(solution)/shard_map/psum | solution.py:79
  1384.2 206.2 %all-reduce.13.cloned.1.call-start = ((), (), s32[]{:S(2)}) async-start(), calls=%async_computation.28 | async-start | bytes 4194304 | tf_op jit(solution)/shard_map/psum | solution.py:79
  1611.4 52.1 %all-to-all-start.9 = ((bf16[4,256,1024]{1,2,0:T(8,128)(2,1)}), bf16[4,256,1024]{1,2,0:T(8,128)(2,1)S(1)}, u32[]{:S(2)}, u32[]{:S(2)}) async-start(bf16[4,256,1024]{1,2,0:T(8,128)(2,1)} %copy.127), calls=%async_computation.13 | async-start | bytes 4194304 | tf_op jit(solution)/shard_map/all_to_all | solution.py:329
  1615.0 135.1 %reduce-scatter.14.cloned.1.call-start = ((), (), s32[]{:S(2)}) async-start(), calls=%async_computation.29 | async-start | bytes 9437184 | tf_op jit(solution)/shard_map/reduce_scatter | solution.py:333
  (69 other events, 2676.3 us)
Sparse Core Ops, SparseCore 0:
  11.5 72.1 all-gather.8
  87.2 57.2 all-gather.10
  147.8 77.3 all-gather.12
  228.5 76.0 all-gather.14
  411.0 155.8 reduce-scatter.5
  569.8 181.9 reduce-scatter.11
  754.7 184.2 reduce-scatter.9
  942.0 142.4 reduce-scatter.7
  1086.6 21.6 all-gather.16
  1110.8 27.8 all-gather.20
  1141.4 27.8 all-gather.18
  1249.3 84.6 all-reduce.8
  1384.4 85.4 all-reduce.10
  1504.9 85.4 all-reduce.12
  1679.3 70.7 reduce-scatter.13
where the time goes:
time: 1770 us; the launch traced here: 1760 us
  waiting for transfers between devices  1260 us (71%)
  matrix products  205 us (12%)
  blocking collectives  145 us (8%)
  local copies, waits for them, and re-layouts  59.3 us (3%)
  other arithmetic  42.9 us (2%)
  starting transfers between devices  37.1 us (2%)
    psum x3, waiting for transfers between devices, orthogonalize(): lax.psum(jnp.dot(current, current.T, precision=highest).astype(jnp.bfloat...  256 us
    reduce_scatter x1, waiting for transfers between devices, per_device(): lax.psum_scatter(grad_up, ('seq', 'shard'), scatter_dimension=0, tiled=True)  185 us
    reduce_scatter x1, waiting for transfers between devices, per_device(): lax.psum_scatter(grad_down, ('seq', 'shard'), scatter_dimension=0, tiled=...  183 us
    reduce_scatter x1, waiting for transfers between devices, per_device(): lax.psum_scatter(grad_out, ('seq', 'shard'), scatter_dimension=0, tiled=T...  143 us
    reduce_scatter x1, waiting for transfers between devices, per_device(): lax.psum_scatter(grad_qkv, ('seq', 'shard'), scatter_dimension=0, tiled=T...  132 us
    all_gather x1, waiting for transfers between devices, per_device(): lax.all_gather(w_up.astype(jnp.bfloat16), ('seq', 'shard'), axis=0, tiled...  78.4 us
    all_gather x1, waiting for transfers between devices, per_device(): lax.all_gather(w_down.astype(jnp.bfloat16), ('seq', 'shard'), axis=0, til...  74.6 us
    all_to_all x1, blocking collectives, per_device(): lax.all_to_all(for_sending(chosen), 'seq', split_axis=1, concat_axis=0, t...  53.1 us
  transfers between devices with their start and end apart: 24, of which 21 were waited for; matrix products, arithmetic and copies ran while one was open for 6% of the time, Pallas kernels for 0%

commit v1 on v0

v1 whole, which is shorter than its diff:
```python
import functools
import math

import jax
import jax.numpy as jnp
from jax import lax
from jax.experimental import pallas as pl
from jax.experimental.pallas import tpu as pltpu
from jax.sharding import PartitionSpec as P

D = 1024
H = 16
HD = 64
FF = 4096
VEC = 12 * D

ca, cb, cc = (3.4445, -4.775, 2.0315)
momentum_decay = 0.9
matrix_rate = 0.1
vector_rate = 0.2
f32 = jnp.float32
b16 = jnp.bfloat16


def layer_norm(values, gain_vec, shift_vec):
    center = values - jnp.mean(values, axis=-1, keepdims=True)
    spread = jnp.mean(center * center, axis=-1, keepdims=True)
    return center * lax.rsqrt(spread + 1e-05) * gain_vec + shift_vec


def normed(values):
    center = values - jnp.mean(values, axis=-1, keepdims=True)
    spread = jnp.mean(center * center, axis=-1, keepdims=True)
    return center * lax.rsqrt(spread + 1e-05)


def gelu_tanh(values):
    return jax.nn.gelu(values, approximate=True)


def dot(a, b):
    return jnp.dot(a, b, preferred_element_type=f32)


def dot_nt(a, b):
    return lax.dot_general(a, b, (((1,), (1,)), ((), ())), preferred_element_type=f32)


def dot_tn(a, b):
    return lax.dot_general(a, b, (((0,), (0,)), ((), ())), preferred_element_type=f32)


def spans(total):
    rows = 128
    reach = total // 2
    out = []
    for begin in range(0, total, rows):
        first = max(0, begin - reach + 1) // 128 * 128
        out.append((begin, rows, first, begin + rows - first))
    return out


def probabilities(q, k, seg_q, seg_k, slope, offset):
    scores = dot_nt(q, k) * HD ** (-0.5)
    shape = scores.shape
    distance = offset + lax.broadcasted_iota(jnp.int32, shape, 0) - lax.broadcasted_iota(
        jnp.int32, shape, 1
    )
    scores = scores - slope * distance.astype(f32)
    scores = jnp.where((distance >= 0) & (seg_q == seg_k), scores, -1e30)
    terms = jnp.exp(scores - jnp.max(scores, axis=-1, keepdims=True))
    return terms * (1.0 / jnp.sum(terms, axis=-1, keepdims=True))


def attend_kernel(slopes, seg_col, seg_row, q, k, v, out):
    pair = pl.program_id(0)
    for j in range(2):
        cols = slice(j * HD, (j + 1) * HD)
        slope = slopes[2 * pair + j]
        for begin, rows, first, wide in spans(q.shape[0]):
            keys = slice(first, first + wide)
            probs = probabilities(
                q[begin : begin + rows, cols],
                k[keys, cols],
                seg_col[begin : begin + rows, :],
                seg_row[:, keys],
                slope,
                begin - first,
            )
            out[begin : begin + rows, cols] = dot(probs.astype(b16), v[keys, cols]).astype(b16)


def attend_back_kernel(slopes, seg_col, seg_row, q, k, v, g, dq, dk, dv, k_acc, v_acc):
    pair = pl.program_id(0)
    k_acc[...] = jnp.zeros_like(k_acc)
    v_acc[...] = jnp.zeros_like(v_acc)
    for j in range(2):
        cols = slice(j * HD, (j + 1) * HD)
        slope = slopes[2 * pair + j]
        for begin, rows, first, wide in spans(q.shape[0]):
            keys = slice(first, first + wide)
            q_block = q[begin : begin + rows, cols]
            g_block = g[begin : begin + rows, cols]
            probs = probabilities(
                q_block,
                k[keys, cols],
                seg_col[begin : begin + rows, :],
                seg_row[:, keys],
                slope,
                begin - first,
            )
            v_acc[keys, cols] += dot_tn(probs.astype(b16), g_block)
            grad_probs = dot_nt(g_block, v[keys, cols])
            inner = jnp.sum(probs * grad_probs, axis=-1, keepdims=True)
            grad_scores = (probs * (grad_probs - inner) * HD ** (-0.5)).astype(b16)
            dq[begin : begin + rows, cols] = dot(grad_scores, k[keys, cols]).astype(b16)
            k_acc[keys, cols] += dot_tn(grad_scores, q_block)
    dk[...] = k_acc[...].astype(b16)
    dv[...] = v_acc[...].astype(b16)


def attention_specs(total, pairs):
    col = pl.BlockSpec((total, 1), lambda p: (0, 0))
    row = pl.BlockSpec((1, total), lambda p: (0, 0))
    parts = [
        pl.BlockSpec((total, 2 * HD), lambda p, base=base: (0, base * pairs + p))
        for base in range(3)
    ]
    return [pl.BlockSpec(memory_space=pltpu.SMEM), col, row] + parts


def attend(slopes, seg, qkv):
    total = qkv.shape[0]
    wide = qkv.shape[1] // 3
    pairs = wide // (2 * HD)
    return pl.pallas_call(
        attend_kernel,
        grid=(pairs,),
        out_shape=jax.ShapeDtypeStruct((total, wide), b16),
        in_specs=attention_specs(total, pairs),
        out_specs=pl.BlockSpec((total, 2 * HD), lambda p: (0, p)),
        compiler_params=pltpu.CompilerParams(vmem_limit_bytes=24 * 2**20),
    )(slopes, seg.reshape(total, 1), seg.reshape(1, total), qkv, qkv, qkv)


def attend_back(slopes, seg, qkv, grad):
    total = qkv.shape[0]
    wide = qkv.shape[1] // 3
    pairs = wide // (2 * HD)
    pair_spec = pl.BlockSpec((total, 2 * HD), lambda p: (0, p))
    part = jax.ShapeDtypeStruct((total, wide), b16)
    return pl.pallas_call(
        attend_back_kernel,
        grid=(pairs,),
        out_shape=(part, part, part),
        in_specs=attention_specs(total, pairs) + [pair_spec],
        out_specs=(pair_spec, pair_spec, pair_spec),
        scratch_shapes=[pltpu.VMEM((total, 2 * HD), f32), pltpu.VMEM((total, 2 * HD), f32)],
        compiler_params=pltpu.CompilerParams(vmem_limit_bytes=24 * 2**20),
    )(slopes, seg.reshape(total, 1), seg.reshape(1, total), qkv, qkv, qkv, grad)


def shift_seq(array, groups, k):
    return lax.ppermute(array, "seq", [(i, (i + k) % groups) for i in range(groups)])


def flip_shard(array, shards, bit):
    return lax.ppermute(array, "shard", [(i, i ^ (1 << bit)) for i in range(shards)])


def gather_seq(array, groups, z, axis):
    size = array.shape[axis]
    shape = list(array.shape)
    shape[axis] = size * groups
    full = jnp.zeros(shape, array.dtype)
    full = lax.dynamic_update_slice_in_dim(full, array, z * size, axis)
    for k in range(1, groups):
        piece = shift_seq(array, groups, k)
        full = lax.dynamic_update_slice_in_dim(full, piece, (z - k) % groups * size, axis)
    return full


def reduce_seq(array, groups, z):
    size = array.shape[0] // groups
    total = lax.dynamic_slice_in_dim(array, z * size, size, 0)
    for k in range(1, groups):
        block = lax.dynamic_slice_in_dim(array, (z + k) % groups * size, size, 0)
        total = total + shift_seq(block.astype(b16), groups, k).astype(f32)
    return total


def gather_seq_line(array, groups, z):
    right, left = [array], [array]
    for _ in range(groups - 1):
        right.append(lax.ppermute(right[-1], "seq", [(i, i + 1) for i in range(groups - 1)]))
        left.append(lax.ppermute(left[-1], "seq", [(i + 1, i) for i in range(groups - 1)]))
    pieces = [array]
    for k in range(1, groups):
        pieces.append(jnp.where(z >= k, right[k], left[groups - k]))
    return pieces


def halve(array, shards, s, bits, order, keep_first=None):
    left = list(bits)
    out = array
    for b in order:
        ax = left.index(b)
        mine = (s >> b) & 1
        keep = lax.dynamic_index_in_dim(out, mine, ax, False)
        give = lax.dynamic_index_in_dim(out, 1 - mine, ax, False)
        got = flip_shard(give, shards, b)
        left.pop(ax)
        out = keep.astype(f32) + got.astype(f32)
        if left:
            out = out.astype(b16)
    return out


def pad_to(array, wide):
    return jnp.pad(array, ((0, 0), (0, wide - array.shape[1])))


def per_device(
    tokens_in,
    out_grad,
    segments,
    w_qkv,
    w_out,
    w_up,
    w_down,
    vectors,
    mom_qkv,
    mom_out,
    mom_up,
    mom_down,
    mom_vectors,
):
    groups = lax.axis_size("seq")
    shards = lax.axis_size("shard")
    z = lax.axis_index("seq")
    s = lax.axis_index("shard")
    length = tokens_in.shape[1]
    total = length * groups
    rows = w_qkv.shape[0]
    owners = shards // 4
    part_d = D // groups
    part_f = FF // groups
    wide = part_f // owners
    chunk = vectors.shape[0]

    def columns_of(matrix, parts):
        split = matrix.astype(b16).reshape(rows, parts, groups, -1)
        return split.transpose(2, 0, 1, 3).reshape(groups, rows, -1)

    lanes = min(chunk, 128)
    vec_rows = chunk // lanes
    vec_block = jnp.pad(
        vectors.astype(b16).reshape(vec_rows, lanes), ((0, rows - vec_rows), (0, 128 - lanes))
    )
    send_a = jnp.concatenate(
        [columns_of(w_qkv, 3), jnp.broadcast_to(vec_block, (groups, rows, 128))], axis=2
    )
    got_a = lax.all_to_all(send_a, "seq", 0, 0)
    send_b = jnp.concatenate(
        [
            jnp.broadcast_to(w_out.astype(b16), (groups, rows, D)),
            columns_of(w_up, 1),
            columns_of(w_down, 1),
        ],
        axis=2,
    )
    residual = gather_seq(tokens_in[0], groups, z, 0).astype(f32)
    all_a = lax.all_gather(got_a, "shard", axis=1).reshape(groups * shards, rows, -1)
    part_qkv = all_a[:, :, : 3 * part_d].reshape(D, 3 * part_d)
    full_vec = all_a[:, :vec_rows, 3 * part_d : 3 * part_d + lanes].reshape(VEC).astype(f32).reshape(12, D)
    send_b, got_a = lax.optimization_barrier((send_b, got_a))
    got_b = lax.all_to_all(send_b, "seq", 0, 0)
    all_b = lax.all_gather(got_b, "shard", axis=1).reshape(D, -1)
    full_out = all_b[:, :D]
    part_up = all_b[:, D : D + part_f]
    part_down = all_b[:, D + part_f :]

    gain_one, shift_one, bias_query, bias_value, bias_out, gain_two, shift_two = (
        full_vec[i] for i in range(7)
    )
    bias_up = lax.dynamic_slice_in_dim(full_vec[7:11].reshape(FF), z * part_f, part_f, 0)
    bias_down = full_vec[11]
    part_bias = jnp.concatenate(
        [
            lax.dynamic_slice_in_dim(bias_query, z * part_d, part_d, 0),
            jnp.zeros((part_d,), f32),
            lax.dynamic_slice_in_dim(bias_value, z * part_d, part_d, 0),
        ]
    )

    normed_one = normed(residual)
    hidden_one = (normed_one * gain_one + shift_one).astype(b16)
    qkv = (dot(hidden_one, part_qkv) + part_bias).astype(b16)
    head_count = part_d // HD
    heads = (z * head_count + jnp.arange(head_count)).astype(f32)
    slopes = jnp.exp2(-8.0 * (heads + 1.0) / H)
    attended_part = attend(slopes, segments[0], qkv)
    attended = gather_seq(attended_part, groups, z, 1)
    middle = residual + dot(attended, full_out) + bias_out
    normed_two = normed(middle)
    hidden_two = (normed_two * gain_two + shift_two).astype(b16)
    before = dot(hidden_two, part_up) + bias_up
    active = gelu_tanh(before).astype(b16)
    cotangent = gather_seq(out_grad[0], groups, z, 0)
    own_upstream = out_grad[0].astype(f32)

    grad_active = dot(cotangent, part_down)
    grad_before = jax.vjp(gelu_tanh, before)[1](grad_active)[0]
    grad_before_b = grad_before.astype(b16)
    hidden_two_share = dot_nt(grad_before_b, part_up)
    grad_hidden_two = reduce_seq(hidden_two_share, groups, z)
    own_middle = lax.dynamic_slice_in_dim(middle, z * length, length, 0)
    middle_part = jax.vjp(lambda m: layer_norm(m, gain_two, shift_two), own_middle)[1](
        grad_hidden_two
    )[0]
    grad_middle = own_upstream + middle_part
    grad_middle_b = grad_middle.astype(b16)
    grad_attended = dot_nt(grad_middle_b, full_out).astype(b16)

    def to_columns(array):
        blocks = array.reshape(length, groups, part_d).transpose(1, 0, 2)
        return lax.all_to_all(blocks, "seq", 0, 0).reshape(total, part_d)

    head_grad = to_columns(grad_attended)
    middle_cols = to_columns(grad_middle_b)
    grad_q, grad_k, grad_v = attend_back(slopes, segments[0], qkv, head_grad)
    grad_mixed = jnp.concatenate([grad_q, grad_k, grad_v], axis=1)
    hidden_one_share = dot_nt(grad_mixed, part_qkv)

    block_share = dot_nt(active, part_down)
    block_rows = (reduce_seq(block_share, groups, z) + own_middle + bias_down).astype(b16)
    grad_hidden_one = reduce_seq(hidden_one_share, groups, z)
    own_residual = tokens_in[0].astype(f32)
    input_part = jax.vjp(lambda m: layer_norm(m, gain_one, shift_one), own_residual)[1](
        grad_hidden_one
    )[0]
    grad_rows = grad_middle + input_part

    def placed(values, width):
        return lax.dynamic_update_slice_in_dim(jnp.zeros((width,), f32), values, z * values.shape[0], 0)

    share_vec = jnp.concatenate(
        [
            jnp.sum(hidden_one_share * normed_one, axis=0),
            jnp.sum(hidden_one_share, axis=0),
            placed(jnp.sum(grad_q.astype(f32), axis=0), D),
            placed(jnp.sum(grad_v.astype(f32), axis=0), D),
            jnp.sum(grad_middle, axis=0),
            jnp.sum(hidden_two_share * normed_two, axis=0),
            jnp.sum(hidden_two_share, axis=0),
            placed(jnp.sum(grad_before, axis=0), FF),
            jnp.sum(own_upstream, axis=0),
        ]
    )
    vec_area = jnp.pad(
        share_vec.astype(b16).reshape(groups * shards, 1, chunk), ((0, 0), (0, rows - 1), (0, 0))
    ).reshape(D, chunk)

    low = s & 1
    pairs = (
        (hidden_one, grad_mixed),
        (attended, middle_cols),
        (hidden_two, grad_before_b),
        (cotangent, active),
    )

    def half(bit):
        blocks = []
        for index, (left, right) in enumerate(pairs):
            size = right.shape[1] // owners
            for high in range(owners // 2):
                cut = lax.dynamic_slice_in_dim(right, (2 * high + bit) * size, size, 1)
                block = dot_tn(left, cut).astype(b16)
                if index == 1 and high == 0:
                    block = jnp.concatenate(
                        [block, jnp.where(bit == 0, vec_area, jnp.zeros_like(vec_area))], axis=1
                    )
                blocks.append(pad_to(block, wide))
        return jnp.stack(blocks)

    got = flip_shard(half(1 - low), shards, 0)
    summed = (half(low).astype(f32) + got.astype(f32)).astype(b16)
    bit_count = shards.bit_length() - 1
    bits = list(range(bit_count - 1, 0, -1))
    summed = summed.reshape([2] * len(bits) + [D, wide])
    up_order = bits[::-1]
    other_order = up_order[len(bits) // 2 :] + up_order[: len(bits) // 2]
    halves = [
        halve(summed[..., : D // 2, :], shards, s, bits, up_order),
        halve(summed[..., D // 2 :, :], shards, s, bits, other_order),
    ]
    own_grad = jnp.concatenate(halves, axis=0)
    own_grad_b = own_grad.astype(b16)

    def blocks_of(matrix, parts):
        split = matrix.reshape(rows, parts, groups, -1).transpose(0, 2, 1, 3)
        split = split.reshape(rows, groups, owners, -1)
        return jnp.pad(split, ((0, 0), (0, 0), (0, 0), (0, wide - split.shape[3])))

    mom_blocks = jnp.stack(
        [
            blocks_of(mom_qkv.astype(b16), 3),
            blocks_of(mom_out.astype(b16), 1),
            blocks_of(mom_up.astype(b16), 1),
            blocks_of(mom_down.astype(b16), 1),
        ],
        axis=2,
    )
    mom_blocks = mom_blocks.transpose(1, 2, 3, 0, 4).reshape(groups * shards, rows, wide)
    mom_blocks, _ = lax.optimization_barrier((mom_blocks, attended))
    own_mom = lax.all_to_all(mom_blocks, ("seq", "shard"), 0, 0).reshape(D, wide)
    column = lax.broadcasted_iota(jnp.int32, (D, wide), 1)
    is_out = s // owners == 1
    held = jnp.where(is_out & (column >= part_d // owners), 0.0, momentum_decay * own_mom.astype(f32) + own_grad)

    pieces = gather_seq_line(held.astype(b16), groups, z)
    grad_back = lax.all_to_all(
        own_grad_b.reshape(groups * shards, rows, wide), ("seq", "shard"), 0, 0
    )
    columns_here = jnp.concatenate(pieces, axis=1)
    gram = dot_nt(columns_here, columns_here)
    for b in range(owners.bit_length() - 1):
        mine = gram.astype(b16)
        gram = mine.astype(f32) + flip_shard(mine, shards, b).astype(f32)
    factor = 1.0 / (jnp.sqrt(jnp.trace(gram)) + 1e-07)

    def mul(x, y):
        return dot(x.astype(b16), y.astype(b16))

    a_zero = gram * (factor * factor)
    r_zero = cb * a_zero + cc * mul(a_zero, a_zero)
    r_zero_b = r_zero.astype(b16)
    once = ca * a_zero + mul(a_zero, r_zero_b)
    a_one = ca * once + mul(once, r_zero_b)
    a_one_b = a_one.astype(b16)
    r_one_b = (cb * a_one + cc * mul(a_one_b, a_one_b)).astype(b16)
    span = D // groups
    lead = lax.dynamic_slice_in_dim(a_one, z * span, span, 0)
    lead = ca * lead + mul(lead, r_one_b)
    lead = ca * lead + mul(lead, r_one_b)
    square = mul(lead, a_one_b)
    square = ca * square + mul(square, r_one_b)
    square = ca * square + mul(square, r_one_b)
    row_at = lax.broadcasted_iota(jnp.int32, (span, D), 0) + z * span
    unit = jnp.where(row_at == lax.broadcasted_iota(jnp.int32, (span, D), 1), ca, 0.0)
    last = unit + cb * lead + cc * square
    last = ca * last + mul(last, r_one_b)
    last = ca * last + mul(last, r_zero_b)
    last = (last * factor).astype(b16)
    result = dot(last, columns_here).astype(b16).reshape(shards, rows, groups * wide)
    result = lax.all_to_all(result, "shard", 0, 0)
    result = result.reshape(shards, rows, groups, wide)
    result = jnp.stack(
        [lax.dynamic_index_in_dim(result, (z - j) % groups, 2, False) for j in range(groups)], axis=2
    )
    ortho = result.reshape(4, owners, rows, groups, wide)
    grad_back = grad_back.reshape(groups, 4, owners, rows, wide)

    def rows_of(blocks, parts, width):
        cut = blocks[..., : width // groups // owners].reshape(rows, groups, parts, -1)
        return cut.transpose(0, 2, 1, 3).reshape(rows, width).astype(f32)

    widths = (3 * D, D, FF, FF)
    part_counts = (3, 1, 1, 1)
    weights = (w_qkv, w_out, w_up, w_down)
    moments = (mom_qkv, mom_out, mom_up, mom_down)
    grads, news, nexts = [], [], []
    for m in range(4):
        grad = rows_of(grad_back[:, m].transpose(2, 0, 1, 3), part_counts[m], widths[m])
        update = rows_of(ortho[m].transpose(1, 2, 0, 3), part_counts[m], widths[m])
        grads.append(grad)
        nexts.append(momentum_decay * moments[m] + grad)
        news.append(weights[m] - matrix_rate * 0.2 * math.sqrt(widths[m]) * update)
    grad_vec = jnp.sum(grad_back[:, 1, 0, 0, part_d // owners :].astype(f32), axis=0)
    next_vec = momentum_decay * mom_vectors + grad_vec
    new_vec = vectors - vector_rate / math.sqrt(total * shards) * next_vec
    return (
        block_rows[None],
        grad_rows[None],
        *grads,
        grad_vec,
        *news,
        new_vec,
        *nexts,
        next_vec,
    )


def solution(mesh):
    tokens = P("shard", "seq", None)
    matrix = P(("seq", "shard"), None)
    vector = P(("seq", "shard"))
    five = (matrix,) * 4 + (vector,)
    return jax.shard_map(
        per_device,
        mesh=mesh,
        in_specs=(tokens, tokens, P("shard", None)) + five + five,
        out_specs=(tokens, tokens) + five + five + five,
        check_vma=False,
    )
```

time: 1770 us -> 582 us (0.33)
  waiting for transfers between devices: 1260 us -> 215 us
  matrix products: 205 us -> 62.8 us
  blocking collectives: 145 us -> 67.8 us
  starting transfers between devices: 37.1 us -> 89.9 us
    reduce_scatter x5 -> x0, waiting for transfers between devices: 660 us -> none  [the longest x1 185 us: per_device(): lax.psum_scatter(grad_up, ('seq', 'shard'), scatter_dimension=0, tiled=True)]
    psum x3 -> x0, waiting for transfers between devices: 256 us -> none  [orthogonalize(): lax.psum(jnp.dot(current, current.T, precision=highest).astype(jnp.bfloat...]
    all_gather x7 -> x2, waiting for transfers between devices: 251 us -> 0.04 us  [the longest x1 0.02 us: per_device(): all_b = lax.all_gather(got_b, 'shard', axis=1).reshape(D, -1)]
    ppermute x0 -> x30, waiting for transfers between devices: none -> 174 us  [the longest x18 76.4 us: shift_seq(): lax.ppermute(array, 'seq', [(i, (i + k) % groups) for i in range(groups)])]
    dot_general x34 -> x28, matrix products: 205 us -> 62.8 us  [the longest x15 39.6 us: dot(): return jnp.dot(a, b, preferred_element_type=f32)]
    ppermute x0 -> x30, starting transfers between devices: none -> 73.4 us  [the longest x18 50.2 us: shift_seq(): lax.ppermute(array, 'seq', [(i, (i + k) % groups) for i in range(groups)])]
    all_gather x2 -> x0, blocking collectives: 53.3 us -> none  [the longest x1 43.5 us: per_device(): lax.all_gather(vectors.astype(jnp.bfloat16), ('seq', 'shard'), axis=0, ti...]
    all_to_all x9 -> x4, waiting for transfers between devices: 88.6 us -> 40.7 us  [the longest x1 26.2 us: per_device(): lax.all_to_all(mom_blocks, ('seq', 'shard'), 0, 0).reshape(D, wide)]
  transfers between devices with their start and end apart: 24 -> 36, of which waited for: 21 -> 19; matrix products, arithmetic and copies ran while one was open for 6% -> 8% of each run, Pallas kernels for 0% -> 3%
where the time goes in v1:
time: 582 us; the launch traced here: 575 us
  waiting for transfers between devices  215 us (37%)
  starting transfers between devices  89.9 us (15%)
  blocking collectives  67.8 us (12%)
  matrix products  62.8 us (11%)
  local copies, waits for them, and re-layouts  58.4 us (10%)
  other arithmetic  46.7 us (8%)
  Pallas kernels  17.4 us (3%)
  between operations  16.7 us (3%)
    ppermute x18, waiting for transfers between devices, shift_seq(): lax.ppermute(array, 'seq', [(i, (i + k) % groups) for i in range(groups)])  76.4 us
    ppermute x3, waiting for transfers between devices, gather_seq_line(): lax.ppermute(right[-1], 'seq', [(i, i + 1) for i in range(groups - 1)])  58.7 us
    ppermute x18, starting transfers between devices, shift_seq(): lax.ppermute(array, 'seq', [(i, (i + k) % groups) for i in range(groups)])  50.2 us
    dot_general x15, matrix products, dot(): return jnp.dot(a, b, preferred_element_type=f32)  39.6 us
    ppermute x6, waiting for transfers between devices, flip_shard(): lax.ppermute(array, 'shard', [(i, i ^ 1 << bit) for i in range(shards)])  34.1 us
    all_to_all x1, blocking collectives, per_device(): lax.all_to_all(own_grad_b.reshape(groups * shards, rows, wide), ('seq', '...  31 us
    all_to_all x1, waiting for transfers between devices, per_device(): lax.all_to_all(mom_blocks, ('seq', 'shard'), 0, 0).reshape(D, wide)  26.2 us
    all_to_all x1, blocking collectives, per_device(): got_b = lax.all_to_all(send_b, 'seq', 0, 0)  22.4 us
  transfers between devices with their start and end apart: 36, of which 19 were waited for; matrix products, arithmetic and copies ran while one was open for 8% of the time, Pallas kernels for 3%

profile of v1, /device:TPU:0, one launch (start us, length us, event | category | flops | bytes accessed | tf_op | source)
XLA Modules:
  0.0 574.6 jit_solution(9199088673189235634)
XLA Ops:
  9.6 14.4 %all_to_all.35 = bf16[4,32,896]{2,1,0:T(8,128)(2,1)} all-to-all(bf16[4,32,896]{2,1,0:T(8,128)(2,1)S(1)} %pad_maximum_fusion.6), channel_id=1, replica_groups=mesh['seq'=4,'shard'=8] {'seq'}, dimensions={0} | all-to-all | bytes 458752 | tf_op jit(solution)/shard_map/all_to_all | solution.py:263
  25.3 22.4 %all_to_all.36 = bf16[4,32,3072]{2,1,0:T(8,128)(2,1)S(1)} all-to-all(bf16[4,32,3072]{2,1,0:T(8,128)(2,1)S(1)} %copy.124), channel_id=1, replica_groups=mesh['seq'=4,'shard'=8] {'seq'}, dimensions={0} | all-to-all | bytes 1572864 | tf_op jit(solution)/shard_map/all_to_all | solution.py:277
  61.2 16.0 %collective-permute-done.9 = bf16[128,1024]{1,0:T(8,128)(2,1)S(1)} collective-permute-done((bf16[128,1024]{1,0:T(8,128)(2,1)S(1)}, bf16[128,1024]{1,0:T(8,128)(2,1)S(1)}, u32[]{:S(2)}, u32[]{:S(2)}) %collective-permute-start.9) | collective-permute-done | bytes 262176 | tf_op jit(solution)/shard_map/ppermute | solution.py:164
  85.4 6.7 %shard_map.260 = bf16[512,256]{1,0:T(8,128)(2,1)S(1)} custom-call(f32[4]{0:T(128)S(1)} %multiply_exponential_fusion.slopes, s32[512,1]{1,0:T(8,128)S(1)} %copy.123.seg_col, s32[1,512]{1,0:T(1,128)S(1)} %copy-done, bf16[512,768]{1,0:T(8,128)(2,1)S(1)} %add_convert_fusion.4.q.k.v, bf16[512,768]{1,0:T(8,128)(2,1)S(1)} %add_convert_fusion.4.q.k.v, ...), custom_call_target="tpu_custom_call" | custom-call | tf_op jit(solution)/shard_map/pallas_call | solution.py:136
  92.1 12.9 %collective-permute-start.3 = (bf16[512,256]{1,0:T(8,128)(2,1)S(1)}, bf16[512,256]{1,0:T(8,128)(2,1)S(1)}, u32[]{:S(2)}, u32[]{:S(2)}) collective-permute-start(bf16[512,256]{1,0:T(8,128)(2,1)S(1)} %shard_map.260), channel_id=1, source_target_pairs={{0,8},{8,16},{16,24},{24,0},{1,9},{9,17},{17,25},{25,1},{2,10},{10... | collective-permute-start | bytes 786440 | tf_op jit(solution)/shard_map/ppermute | solution.py:164
  112.8 6.1 %collective-permute-done.4 = bf16[512,256]{1,0:T(8,128)(2,1)S(1)} collective-permute-done((bf16[512,256]{1,0:T(8,128)(2,1)S(1)}, bf16[512,256]{1,0:T(8,128)(2,1)S(1)}, u32[]{:S(2)}, u32[]{:S(2)}) %collective-permute-start.4) | collective-permute-done | bytes 262176 | tf_op jit(solution)/shard_map/ppermute | solution.py:164
  133.2 10.6 %collective-permute-start.14 = (bf16[128,1024]{1,0:T(8,128)(2,1)S(1)}, bf16[128,1024]{1,0:T(8,128)(2,1)S(1)}, u32[]{:S(2)}, u32[]{:S(2)}) collective-permute-start(bf16[128,1024]{1,0:T(8,128)(2,1)S(1)} %get-tuple-element.50), channel_id=1, source_target_pairs={{0,24},{8,0},{16,8},{24,16},{1,25},{9,1},{17,9},{25,17},{2,26},{10... | collective-permute-start | bytes 786440 | tf_op jit(solution)/shard_map/ppermute | solution.py:164
  150.6 7.6 %collective-permute-start.6 = (bf16[128,1024]{1,0:T(8,128)(2,1)S(1)}, bf16[128,1024]{1,0:T(8,128)(2,1)S(1)}, u32[]{:S(2)}, u32[]{:S(2)}) collective-permute-start(bf16[128,1024]{1,0:T(8,128)(2,1)S(1)} %get-tuple-element.52), channel_id=1, source_target_pairs={{0,8},{8,16},{16,24},{24,0},{1,9},{9,17},{17,25},{25,1},{2,10},{10... | collective-permute-start | bytes 786440 | tf_op jit(solution)/shard_map/ppermute | solution.py:164
  158.3 18.6 %collective-permute-done.13 = bf16[128,1024]{1,0:T(8,128)(2,1)S(1)} collective-permute-done((bf16[128,1024]{1,0:T(8,128)(2,1)S(1)}, bf16[128,1024]{1,0:T(8,128)(2,1)S(1)}, u32[]{:S(2)}, u32[]{:S(2)}) %collective-permute-start.13) | collective-permute-done | bytes 262176 | tf_op jit(solution)/shard_map/ppermute | solution.py:164
  177.2 9.0 %collective-permute-done.7 = bf16[128,1024]{1,0:T(8,128)(2,1)S(1)} collective-permute-done((bf16[128,1024]{1,0:T(8,128)(2,1)S(1)}, bf16[128,1024]{1,0:T(8,128)(2,1)S(1)}, u32[]{:S(2)}, u32[]{:S(2)}) %collective-permute-start.7) | collective-permute-done | bytes 262176 | tf_op jit(solution)/shard_map/ppermute | solution.py:164
  206.2 10.7 %shard_map.261 = (bf16[512,256]{1,0:T(8,128)(2,1)S(1)}, bf16[512,256]{1,0:T(8,128)(2,1)S(1)}, bf16[512,256]{1,0:T(8,128)(2,1)S(1)}) custom-call(f32[4]{0:T(128)S(1)} %multiply_exponential_fusion.slopes, s32[512,1]{1,0:T(8,128)S(1)} %copy.123.seg_col, s32[1,512]{1,0:T(1,128)S(1)} %copy-done, bf16[512,768]{1,0:T(8,128)(2,1)S(1)} %add_convert_fusion.4.q.k.v, ...), custom_call_target="tpu_custom_call" | custom-call | tf_op jit(solution)/shard_map/pallas_call | solution.py:152
  244.5 21.5 %collective-permute-done.21 = bf16[2,512,512]{2,1,0:T(8,128)(2,1)} collective-permute-done((bf16[2,512,512]{2,1,0:T(8,128)(2,1)S(1)}, bf16[2,512,512]{2,1,0:T(8,128)(2,1)}, u32[]{:S(2)}, u32[]{:S(2)}) %collective-permute-start.21) | collective-permute-done | bytes 1048608 | tf_op jit(solution)/shard_map/ppermute | solution.py:168
  272.4 8.7 %collective-permute-done.22 = bf16[512,512]{1,0:T(8,128)(2,1)S(1)} collective-permute-done((bf16[512,512]{1,0:T(8,128)(2,1)S(1)}, bf16[512,512]{1,0:T(8,128)(2,1)S(1)}, u32[]{:S(2)}, u32[]{:S(2)}) %collective-permute-start.22) | collective-permute-done | bytes 524320 | tf_op jit(solution)/shard_map/ppermute | solution.py:168
  284.2 31.0 %all_to_all.37 = bf16[32,32,512]{2,1,0:T(8,128)(2,1)S(1)} all-to-all(bf16[32,32,512]{2,1,0:T(8,128)(2,1)S(1)} %bitcast.179), channel_id=1, replica_groups=mesh['seq'=4,'shard'=8] {'seq','shard'}, dimensions={0} | all-to-all | bytes 2097152 | tf_op jit(solution)/shard_map/all_to_all | solution.py:422
  359.0 26.2 %all-to-all-done.5 = bf16[32,32,512]{2,1,0:T(8,128)(2,1)} async-done(((bf16[32,32,512]{2,1,0:T(8,128)(2,1)}), bf16[32,32,512]{2,1,0:T(8,128)(2,1)}, u32[]{:S(2)}, u32[]{:S(2)}) %all-to-all-start.5) | async-done | bytes 1048608 | tf_op jit(solution)/shard_map/all_to_all | solution.py:416
  391.3 21.4 %collective-permute-done.23 = bf16[1024,512]{1,0:T(8,128)(2,1)S(1)} collective-permute-done((bf16[1024,512]{1,0:T(8,128)(2,1)S(1)}, bf16[1024,512]{1,0:T(8,128)(2,1)S(1)}, u32[]{:S(2)}, u32[]{:S(2)}) %collective-permute-start.23) | collective-permute-done | bytes 1048608 | tf_op jit(solution)/shard_map/ppermute | solution.py:195
  419.3 19.7 %collective-permute-done.27 = bf16[1024,512]{1,0:T(8,128)(2,1)} collective-permute-done((bf16[1024,512]{1,0:T(8,128)(2,1)S(1)}, bf16[1024,512]{1,0:T(8,128)(2,1)}, u32[]{:S(2)}, u32[]{:S(2)}) %collective-permute-start.27) | collective-permute-done | bytes 1048608 | tf_op jit(solution)/shard_map/ppermute | solution.py:195
  439.0 5.5 collective-permute-start.28
  447.1 17.7 %collective-permute-done.28 = bf16[1024,512]{1,0:T(8,128)(2,1)} collective-permute-done((bf16[1024,512]{1,0:T(8,128)(2,1)}, bf16[1024,512]{1,0:T(8,128)(2,1)}, u32[]{:S(2)}, u32[]{:S(2)}) %collective-permute-start.28) | collective-permute-done | bytes 1048608 | tf_op jit(solution)/shard_map/ppermute | solution.py:195
  480.5 6.9 %collective-permute-done.17 = bf16[128,1024]{1,0:T(8,128)(2,1)} collective-permute-done((bf16[128,1024]{1,0:T(8,128)(2,1)}, bf16[128,1024]{1,0:T(8,128)(2,1)}, u32[]{:S(2)}, u32[]{:S(2)}) %collective-permute-start.17) | collective-permute-done | bytes 262176 | tf_op jit(solution)/shard_map/ppermute | solution.py:164
  487.4 16.3 %collective-permute-done.16 = bf16[128,1024]{1,0:T(8,128)(2,1)} collective-permute-done((bf16[128,1024]{1,0:T(8,128)(2,1)}, bf16[128,1024]{1,0:T(8,128)(2,1)}, u32[]{:S(2)}, u32[]{:S(2)}) %collective-permute-start.16) | collective-permute-done | bytes 262176 | tf_op jit(solution)/shard_map/ppermute | solution.py:164
  508.4 5.7 add_convert_fusion.2
  532.7 5.6 convolution_convert_fusion
  545.4 12.0 %all-to-all-done.6 = bf16[8,32,2048]{2,1,0:T(8,128)(2,1)S(1)} async-done(((bf16[8,32,2048]{2,1,0:T(8,128)(2,1)}), bf16[8,32,2048]{2,1,0:T(8,128)(2,1)S(1)}, u32[]{:S(2)}, u32[]{:S(2)}) %all-to-all-start.6) | async-done | bytes 1048608 | tf_op jit(solution)/shard_map/all_to_all | solution.py:456
  (340 shorter events, 224.7 us)
Async XLA Ops:
  7.2 71.9 %all-gather.5.cloned.1.call-start = ((), (), s32[]{:S(2)}) async-start(), calls=%async_computation.7 | async-start | bytes 2064384 | tf_op jit(solution)/shard_map/all_gather | solution.py:273
  24.0 95.0 %all-gather.7.cloned.1.call-start = ((), (), s32[]{:S(2)}) async-start(), calls=%async_computation.8 | async-start | bytes 7077888 | tf_op jit(solution)/shard_map/all_gather | solution.py:278
  49.4 28.9 %collective-permute-start.1 = (bf16[128,1024]{1,0:T(8,128)(2,1)S(1)}, bf16[128,1024]{1,0:T(8,128)(2,1)S(1)}, u32[]{:S(2)}, u32[]{:S(2)}) collective-permute-start(bf16[128,1024]{1,0:T(8,128)(2,1)S(1)} %bitcast.185), channel_id=1, source_target_pairs={{0,16},{8,24},{16,0},{24,8},{1,17},{9,25},{17,1},{25,9},{2,18},{10... | collective-permute-start | bytes 786440 | tf_op jit(solution)/shard_map/ppermute | solution.py:164
  51.3 27.1 %collective-permute-start.2 = (bf16[128,1024]{1,0:T(8,128)(2,1)S(1)}, bf16[128,1024]{1,0:T(8,128)(2,1)S(1)}, u32[]{:S(2)}, u32[]{:S(2)}) collective-permute-start(bf16[128,1024]{1,0:T(8,128)(2,1)S(1)} %bitcast.186), channel_id=1, source_target_pairs={{0,24},{8,0},{16,8},{24,16},{1,25},{9,1},{17,9},{25,17},{2,26},{10... | collective-permute-start | bytes 786440 | tf_op jit(solution)/shard_map/ppermute | solution.py:164
  53.1 24.1 %collective-permute-start.9 = (bf16[128,1024]{1,0:T(8,128)(2,1)S(1)}, bf16[128,1024]{1,0:T(8,128)(2,1)S(1)}, u32[]{:S(2)}, u32[]{:S(2)}) collective-permute-start(bf16[128,1024]{1,0:T(8,128)(2,1)S(1)} %bitcast.181), channel_id=1, source_target_pairs={{0,8},{8,16},{16,24},{24,0},{1,9},{9,17},{17,25},{25,1},{2,10},{10... | collective-permute-start | bytes 786440 | tf_op jit(solution)/shard_map/ppermute | solution.py:164
  53.6 51.4 %collective-permute-start.10 = (bf16[128,1024]{1,0:T(8,128)(2,1)S(1)}, bf16[128,1024]{1,0:T(8,128)(2,1)S(1)}, u32[]{:S(2)}, u32[]{:S(2)}) collective-permute-start(bf16[128,1024]{1,0:T(8,128)(2,1)S(1)} %bitcast.182), channel_id=1, source_target_pairs={{0,16},{8,24},{16,0},{24,8},{1,17},{9,25},{17,1},{25,9},{2,18},{10... | collective-permute-start | bytes 786440 | tf_op jit(solution)/shard_map/ppermute | solution.py:164
  60.4 47.4 %collective-permute-start.11 = (bf16[128,1024]{1,0:T(8,128)(2,1)S(1)}, bf16[128,1024]{1,0:T(8,128)(2,1)}, u32[]{:S(2)}, u32[]{:S(2)}) collective-permute-start(bf16[128,1024]{1,0:T(8,128)(2,1)S(1)} %bitcast.183), channel_id=1, source_target_pairs={{0,24},{8,0},{16,8},{24,16},{1,25},{9,1},{17,9},{25,17},{2,26},{10... | collective-permute-start | bytes 786440 | tf_op jit(solution)/shard_map/ppermute | solution.py:164
  143.9 33.0 %collective-permute-start.13 = (bf16[128,1024]{1,0:T(8,128)(2,1)S(1)}, bf16[128,1024]{1,0:T(8,128)(2,1)S(1)}, u32[]{:S(2)}, u32[]{:S(2)}) collective-permute-start(bf16[128,1024]{1,0:T(8,128)(2,1)S(1)} %get-tuple-element.51), channel_id=1, source_target_pairs={{0,16},{8,24},{16,0},{24,8},{1,17},{9,25},{17,1},{25,9},{2,18},{10... | collective-permute-start | bytes 786440 | tf_op jit(solution)/shard_map/ppermute | solution.py:164
  143.9 33.0 %collective-permute-start.12 = (bf16[128,1024]{1,0:T(8,128)(2,1)S(1)}, bf16[128,1024]{1,0:T(8,128)(2,1)S(1)}, u32[]{:S(2)}, u32[]{:S(2)}) collective-permute-start(bf16[128,1024]{1,0:T(8,128)(2,1)S(1)} %get-tuple-element.49), channel_id=1, source_target_pairs={{0,8},{8,16},{16,24},{24,0},{1,9},{9,17},{17,25},{25,1},{2,10},{10... | collective-permute-start | bytes 786440 | tf_op jit(solution)/shard_map/ppermute | solution.py:164
  145.9 31.3 %collective-permute-start.8 = (bf16[128,1024]{1,0:T(8,128)(2,1)S(1)}, bf16[128,1024]{1,0:T(8,128)(2,1)S(1)}, u32[]{:S(2)}, u32[]{:S(2)}) collective-permute-start(bf16[128,1024]{1,0:T(8,128)(2,1)S(1)} %get-tuple-element.53), channel_id=1, source_target_pairs={{0,24},{8,0},{16,8},{24,16},{1,25},{9,1},{17,9},{25,17},{2,26},{10... | collective-permute-start | bytes 786440 | tf_op jit(solution)/shard_map/ppermute | solution.py:164
  149.2 37.0 %collective-permute-start.7 = (bf16[128,1024]{1,0:T(8,128)(2,1)S(1)}, bf16[128,1024]{1,0:T(8,128)(2,1)S(1)}, u32[]{:S(2)}, u32[]{:S(2)}) collective-permute-start(bf16[128,1024]{1,0:T(8,128)(2,1)S(1)} %get-tuple-element.54), channel_id=1, source_target_pairs={{0,16},{8,24},{16,0},{24,8},{1,17},{9,25},{17,1},{25,9},{2,18},{10... | collective-permute-start | bytes 786440 | tf_op jit(solution)/shard_map/ppermute | solution.py:164
  150.6 35.6 %collective-permute-start.6 = (bf16[128,1024]{1,0:T(8,128)(2,1)S(1)}, bf16[128,1024]{1,0:T(8,128)(2,1)S(1)}, u32[]{:S(2)}, u32[]{:S(2)}) collective-permute-start(bf16[128,1024]{1,0:T(8,128)(2,1)S(1)} %get-tuple-element.52), channel_id=1, source_target_pairs={{0,8},{8,16},{16,24},{24,0},{1,9},{9,17},{17,25},{25,1},{2,10},{10... | collective-permute-start | bytes 786440 | tf_op jit(solution)/shard_map/ppermute | solution.py:164
  240.6 25.4 %collective-permute-start.21 = (bf16[2,512,512]{2,1,0:T(8,128)(2,1)S(1)}, bf16[2,512,512]{2,1,0:T(8,128)(2,1)}, u32[]{:S(2)}, u32[]{:S(2)}) collective-permute-start(bf16[2,512,512]{2,1,0:T(8,128)(2,1)S(1)} %dynamic-slice_bitcast_fusion), channel_id=1, source_target_pairs={{0,4},{1,5},{2,6},{3,7},{4,0},{5,1},{6,2},{7,3},{8,12},{9,13},{10,... | collective-permute-start | bytes 3145736 | tf_op jit(solution)/shard_map/ppermute | solution.py:168
  243.1 26.3 %collective-permute-start.19 = (bf16[2,512,512]{2,1,0:T(8,128)(2,1)}, bf16[2,512,512]{2,1,0:T(8,128)(2,1)}, u32[]{:S(2)}, u32[]{:S(2)}) collective-permute-start(bf16[2,512,512]{2,1,0:T(8,128)(2,1)} %dynamic-slice_bitcast_fusion.1), channel_id=1, source_target_pairs={{0,2},{1,3},{2,0},{3,1},{4,6},{5,7},{6,4},{7,5},{8,10},{9,11},{10,... | collective-permute-start | bytes 3145736 | tf_op jit(solution)/shard_map/ppermute | solution.py:168
  355.2 30.0 %all-to-all-start.5 = ((bf16[32,32,512]{2,1,0:T(8,128)(2,1)}), bf16[32,32,512]{2,1,0:T(8,128)(2,1)}, u32[]{:S(2)}, u32[]{:S(2)}) async-start(bf16[32,32,512]{2,1,0:T(8,128)(2,1)} %bitcast.180), calls=%async_computation.5 | async-start | bytes 2097152 | tf_op jit(solution)/shard_map/all_to_all | solution.py:416
  387.3 25.4 %collective-permute-start.23 = (bf16[1024,512]{1,0:T(8,128)(2,1)S(1)}, bf16[1024,512]{1,0:T(8,128)(2,1)S(1)}, u32[]{:S(2)}, u32[]{:S(2)}) collective-permute-start(bf16[1024,512]{1,0:T(8,128)(2,1)S(1)} %fusion.20), channel_id=1, source_target_pairs={{0,8},{8,16},{16,24},{1,9},{9,17},{17,25},{2,10},{10,18},{18,26},{... | collective-permute-start | bytes 3145736 | tf_op jit(solution)/shard_map/ppermute | solution.py:195
  390.0 28.0 %collective-permute-start.24 = (bf16[1024,512]{1,0:T(8,128)(2,1)S(1)}, bf16[1024,512]{1,0:T(8,128)(2,1)S(1)}, u32[]{:S(2)}, u32[]{:S(2)}) collective-permute-start(bf16[1024,512]{1,0:T(8,128)(2,1)S(1)} %fusion.20), channel_id=1, source_target_pairs={{8,0},{16,8},{24,16},{9,1},{17,9},{25,17},{10,2},{18,10},{26,18},{... | collective-permute-start | bytes 3145736 | tf_op jit(solution)/shard_map/ppermute | solution.py:196
  412.7 26.3 %collective-permute-start.27 = (bf16[1024,512]{1,0:T(8,128)(2,1)S(1)}, bf16[1024,512]{1,0:T(8,128)(2,1)}, u32[]{:S(2)}, u32[]{:S(2)}) collective-permute-start(bf16[1024,512]{1,0:T(8,128)(2,1)S(1)} %collective-permute-done.23), channel_id=1, source_target_pairs={{0,8},{8,16},{16,24},{1,9},{9,17},{17,25},{2,10},{10,18},{18,26},{... | collective-permute-start | bytes 3145736 | tf_op jit(solution)/shard_map/ppermute | solution.py:195
  418.0 26.4 %collective-permute-start.25 = (bf16[1024,512]{1,0:T(8,128)(2,1)S(1)}, bf16[1024,512]{1,0:T(8,128)(2,1)}, u32[]{:S(2)}, u32[]{:S(2)}) collective-permute-start(bf16[1024,512]{1,0:T(8,128)(2,1)S(1)} %collective-permute-done.24), channel_id=1, source_target_pairs={{8,0},{16,8},{24,16},{9,1},{17,9},{25,17},{10,2},{18,10},{26,18},{... | collective-permute-start | bytes 3145736 | tf_op jit(solution)/shard_map/ppermute | solution.py:196
  439.0 25.8 %collective-permute-start.28 = (bf16[1024,512]{1,0:T(8,128)(2,1)}, bf16[1024,512]{1,0:T(8,128)(2,1)}, u32[]{:S(2)}, u32[]{:S(2)}) collective-permute-start(bf16[1024,512]{1,0:T(8,128)(2,1)} %collective-permute-done.27), channel_id=1, source_target_pairs={{0,8},{8,16},{16,24},{1,9},{9,17},{17,25},{2,10},{10,18},{18,26},{... | collective-permute-start | bytes 3145736 | tf_op jit(solution)/shard_map/ppermute | solution.py:195
  444.5 25.4 %collective-permute-start.26 = (bf16[1024,512]{1,0:T(8,128)(2,1)}, bf16[1024,512]{1,0:T(8,128)(2,1)}, u32[]{:S(2)}, u32[]{:S(2)}) collective-permute-start(bf16[1024,512]{1,0:T(8,128)(2,1)} %collective-permute-done.25), channel_id=1, source_target_pairs={{8,0},{16,8},{24,16},{9,1},{17,9},{25,17},{10,2},{18,10},{26,18},{... | collective-permute-start | bytes 3145736 | tf_op jit(solution)/shard_map/ppermute | solution.py:196
  475.8 29.5 %collective-permute-start.29 = (bf16[1024,1024]{1,0:T(8,128)(2,1)S(1)}, bf16[1024,1024]{1,0:T(8,128)(2,1)}, u32[]{:S(2)}, u32[]{:S(2)}) collective-permute-start(bf16[1024,1024]{1,0:T(8,128)(2,1)S(1)} %convolution_convert_fusion.1), channel_id=1, source_target_pairs={{0,1},{1,0},{2,3},{3,2},{4,5},{5,4},{6,7},{7,6},{8,9},{9,8},{10,11... | collective-permute-start | bytes 6291464 | tf_op jit(solution)/shard_map/ppermute | solution.py:168
  478.7 25.0 %collective-permute-start.16 = (bf16[128,1024]{1,0:T(8,128)(2,1)}, bf16[128,1024]{1,0:T(8,128)(2,1)}, u32[]{:S(2)}, u32[]{:S(2)}) collective-permute-start(bf16[128,1024]{1,0:T(8,128)(2,1)} %get-tuple-element.47), channel_id=1, source_target_pairs={{0,16},{8,24},{16,0},{24,8},{1,17},{9,25},{17,1},{25,9},{2,18},{10... | collective-permute-start | bytes 786440 | tf_op jit(solution)/shard_map/ppermute | solution.py:164
  479.9 23.8 %collective-permute-start.15 = (bf16[128,1024]{1,0:T(8,128)(2,1)}, bf16[128,1024]{1,0:T(8,128)(2,1)}, u32[]{:S(2)}, u32[]{:S(2)}) collective-permute-start(bf16[128,1024]{1,0:T(8,128)(2,1)} %get-tuple-element.45), channel_id=1, source_target_pairs={{0,8},{8,16},{16,24},{24,0},{1,9},{9,17},{17,25},{25,1},{2,10},{10... | collective-permute-start | bytes 786440 | tf_op jit(solution)/shard_map/ppermute | solution.py:164
  (54 other events, 503.9 us)
Sparse Core Ops, SparseCore 0:
  24.1 25.8 all-gather.4
  52.0 45.5 all-gather.6
